TPU v7x, 256 devices: a whole 4x4x8 slice. The times are simulated.
256 devices in a mesh: res: 16 (over x, y_lo, core), seq: 16 (over y_hi, z).
Axes of the slice: x: 4, y: 4 (y_hi: 2, y_lo: 2; y = y_hi * 2 + y_lo), z: 8, core: 2. Of those that a mesh axis runs over, the one named last changes fastest.
Arguments:
- alignment_embedding: bfloat16 [512, 1024, 256], P('seq', 'res'), may hold values from -6 to 6
- standardizer_scaling: float32 [256], replicated, may hold values from 0.1 to 1.9
- standardizer_offset: float32 [256], replicated, may hold values from -1 to 1
- first_map_matrix: bfloat16 [256, 32], replicated, may hold values from -0.375 to 0.375
- first_map_offset: float32 [32], replicated, may hold values from -0.6 to 0.6
- second_map_matrix: bfloat16 [256, 32], replicated, may hold values from -0.375 to 0.375
- second_map_offset: float32 [32], replicated, may hold values from -0.6 to 0.6
- final_map_matrix: bfloat16 [1024, 128], replicated, may hold values from -4 to 4
- final_map_offset: float32 [128], replicated, may hold values from -2 to 2
Outputs:
- pair_update: bfloat16 [1024, 1024, 128], P('res', 'seq')
All inputs are finite; a program needn't handle non-finite values.
Results may differ from a plain program's by a relative error of at most 0.0059.
Values may be sent and summed in bfloat16 or wider, within the bound.
A program may use at most 128 MiB of HBM per device.

v0:
```python
import jax
import jax.numpy as jnp
from jax import lax
from jax.sharding import PartitionSpec as P


def standardize_features(values, standardizer_scaling, standardizer_offset):
    values = values.astype(jnp.float32)
    center = jnp.mean(values, axis=-1, keepdims=True)
    spread = jnp.mean((values - center) ** 2, axis=-1, keepdims=True)
    return (values - center) * lax.rsqrt(
        spread + 1e-05
    ) * standardizer_scaling + standardizer_offset


def linear_map_half(standardized_alignment, coefficient_matrix, offset_vector):
    input_lines = standardized_alignment.reshape(-1, standardized_alignment.shape[-1])
    return (
        jnp.dot(input_lines, coefficient_matrix, preferred_element_type=jnp.float32) + offset_vector
    ).astype(jnp.bfloat16)


def local(
    alignment_embedding,
    standardizer_scaling,
    standardizer_offset,
    first_map_matrix,
    first_map_offset,
    second_map_matrix,
    second_map_offset,
    final_map_matrix,
    final_map_offset,
):
    shard_alignment_rows, shard_positions, feature_width = alignment_embedding.shape
    proj = first_map_matrix.shape[1]
    standardized_alignment = standardize_features(
        alignment_embedding, standardizer_scaling, standardizer_offset
    ).astype(jnp.bfloat16)
    first_factor = linear_map_half(
        standardized_alignment, first_map_matrix, first_map_offset
    ).reshape(shard_alignment_rows, shard_positions * proj)
    second_local = linear_map_half(
        standardized_alignment, second_map_matrix, second_map_offset
    ).reshape(shard_alignment_rows, shard_positions, proj)
    second_major = jnp.transpose(second_local, (0, 2, 1))
    right_all = lax.all_gather(second_major, "res", axis=2, tiled=True)
    right_block = lax.all_to_all(right_all, "seq", split_axis=2, concat_axis=0, tiled=True)
    total_seqs = right_block.shape[0]
    col_local = right_block.shape[2]
    right_cols = right_block.reshape(total_seqs, proj * col_local)
    contract = (((0,), (0,)), ((), ()))
    left_all = lax.all_gather(first_factor, "seq", axis=0, tiled=True)
    outer = lax.dot_general(left_all, right_cols, contract, preferred_element_type=jnp.float32)
    outer_mean = (outer / total_seqs).astype(jnp.bfloat16)
    stacked = outer_mean.reshape(shard_positions, proj * proj, col_local)
    result = (
        lax.dot_general(
            stacked, final_map_matrix, (((1,), (0,)), ((), ())), preferred_element_type=jnp.float32
        )
        + final_map_offset
    )
    return result.astype(jnp.bfloat16)


def solution(mesh):
    return jax.shard_map(
        local,
        mesh=mesh,
        in_specs=(P("seq", "res", None), P(), P(), P(), P(), P(), P(), P(), P()),
        out_specs=P("res", "seq", None),
        check_vma=False,
    )
```

profile of v0, /device:TPU:2, one launch (start us, length us, event | category | flops | bytes accessed | tf_op | source)
XLA Modules:
  0.0 247.2 jit_solution(12462938898248857791)
XLA Ops:
  7.4 0.0 copy-start
  7.4 0.0 copy-start.1
  7.4 0.0 copy-start.5
  7.4 0.0 copy-start.6
  7.4 0.0 copy-start.7
  7.4 0.0 copy-start.2
  7.4 0.0 all-gather.5.cloned.1.call-start
  7.4 1.7 convert_reduce_fusion
  9.1 1.9 fusion.4
  11.0 0.0 copy-done.1
  11.0 0.0 copy-done.5
  11.0 0.0 copy-done.6
  11.0 0.7 fusion.7
  11.8 0.0 copy-done.7
  11.8 0.0 copy-done.2
  11.8 0.4 fusion.3
  12.2 0.2 reshape.36
  12.5 1.7 copy.18
  14.1 0.0 all-gather.5.cloned.1.call-update
  14.1 57.7 %all-gather.5.cloned.1.call-done = bf16[32,32,1024]{1,0,2:T(8,128)(2,1)} async-done(((bf16[32,32,64]{1,0,2:T(8,128)(2,1)}), bf16[32,32,1024]{1,0,2:T(8,128)(2,1)}) %all-gather.5.cloned.1.call-update) | async-done | bytes 2097168 | tf_op jit(solution)/shard_map/all_gather | solution.py:46
  71.8 14.5 %reshape.40 = bf16[16,2,32768]{2,1,0:T(2,128)(2,1)} reshape(bf16[1024,32,32]{2,1,0:T(8,128)(2,1)} %bitcast.25) | data formatting | bytes 4194304
  86.3 0.0 copy-start.3
  86.3 9.7 %all-to-all-start = ((bf16[16,2,32768]{2,1,0:T(2,128)(2,1)}), bf16[16,2,32768]{2,1,0:T(2,128)(2,1)S(1)}, u32[]{:S(2)}, u32[]{:S(2)}) async-start(bf16[16,2,32768]{2,1,0:T(2,128)(2,1)} %reshape.40), calls=%async_computation | async-start | bytes 4194304 | tf_op jit(solution)/shard_map/all_to_all | solution.py:47
  96.0 0.2 all-gather.3.cloned.1.call-start
  96.2 0.0 copy-done.3
  96.2 1.1 fusion.2
  97.3 0.3 copy.17
  97.6 1.2 reshape.35
  98.8 0.0 all-gather.3.cloned.1.call-update
  98.8 53.3 %all-to-all-done = bf16[16,2,32768]{2,1,0:T(2,128)(2,1)S(1)} async-done(((bf16[16,2,32768]{2,1,0:T(2,128)(2,1)}), bf16[16,2,32768]{2,1,0:T(2,128)(2,1)S(1)}, u32[]{:S(2)}, u32[]{:S(2)}) %all-to-all-start) | async-done | bytes 2097184 | tf_op jit(solution)/shard_map/all_to_all | solution.py:47
  152.1 8.9 %reshape.41 = bf16[1024,32,32]{2,1,0:T(8,128)(2,1)} reshape(bf16[16,2,32768]{2,1,0:T(2,128)(2,1)S(1)} %all-to-all-done) | data formatting | bytes 4194304
  161.0 11.5 %copy.20 = bf16[16,32,32,64]{3,2,1,0:T(8,128)(2,1)} copy(bf16[16,32,32,64]{2,1,3,0:T(8,128)(2,1)} %bitcast.22) | data formatting | bytes 4194304 | tf_op jit(solution)/shard_map/all_to_all | solution.py:47
  172.5 5.8 %reshape.37 = bf16[512,2048]{1,0:T(8,128)(2,1)S(1)} reshape(bf16[16,32,32,64]{3,2,1,0:T(8,128)(2,1)} %copy.20) | data formatting | bytes 4194304 | tf_op jit(solution)/shard_map/reshape | solution.py:50
  178.3 17.4 %all-gather.3.cloned.1.call-done = bf16[512,2048]{1,0:T(8,128)(2,1)} async-done(((bf16[32,2048]{1,0:T(8,128)(2,1)}), bf16[512,2048]{1,0:T(8,128)(2,1)}) %all-gather.3.cloned.1.call-update) | async-done | bytes 2097168 | tf_op jit(solution)/shard_map/all_gather | solution.py:52
  195.7 8.4 %multiply_convert_fusion = bf16[2048,2048]{1,0:T(8,128)(2,1)} fusion(bf16[512,2048]{1,0:T(8,128)(2,1)} %all-gather.3.cloned.1.call-done, bf16[512,2048]{1,0:T(8,128)(2,1)S(1)} %reshape.37), kind=kOutput, calls=%fused_computation | convolution fusion | flops 4303355904 | bytes 12582912 | tf_op jit(solution)/shard_map/dot_general | solution.py:53
  204.1 0.0 copy-start.4
  204.1 24.4 %reshape.38 = bf16[64,1024,64]{2,1,0:T(8,128)(2,1)} reshape(bf16[2048,2048]{1,0:T(8,128)(2,1)} %multiply_convert_fusion) | data formatting | bytes 16777216 | tf_op jit(solution)/shard_map/reshape | solution.py:55
  228.5 0.0 copy-done
  228.5 0.0 copy-done.4
  228.5 11.3 %add_convert_fusion = bf16[64,64,128]{2,1,0:T(8,128)(2,1)} fusion(bf16[64,1024,64]{2,1,0:T(8,128)(2,1)} %reshape.38, f32[128]{0:T(128)S(1)} %copy-done.4, bf16[1024,128]{1,0:T(8,128)(2,1)S(1)} %copy-done), kind=kOutput, calls=%fused_computation.13 | convolution fusion | flops 1074790400 | bytes 9699840 | tf_op jit(solution)/shard_map/dot_general | solution.py:57
  (2 shorter events, 0.0 us)
Async XLA Ops:
  7.4 221.1 %copy-start = (bf16[1024,128]{1,0:T(8,128)(2,1)S(1)}, bf16[1024,128]{1,0:T(8,128)(2,1)}, u32[]{:S(2)}) copy-start(bf16[1024,128]{1,0:T(8,128)(2,1)} %param.16) | copy-start | bytes 786436
  7.4 3.6 %copy-start.1 = (bf16[32,64,256]{2,1,0:T(8,128)(2,1)S(1)}, bf16[32,64,256]{2,1,0:T(8,128)(2,1)}, u32[]{:S(2)}) copy-start(bf16[32,64,256]{2,1,0:T(8,128)(2,1)} %param.9) | copy-start | bytes 3145732
  7.4 3.6 %copy-start.5 = (f32[256]{0:T(256)S(1)}, f32[256]{0:T(256)}, u32[]{:S(2)}) copy-start(f32[256]{0:T(256)} %param.11) | copy-start | bytes 3076
  7.4 3.7 %copy-start.6 = (f32[256]{0:T(256)S(1)}, f32[256]{0:T(256)}, u32[]{:S(2)}) copy-start(f32[256]{0:T(256)} %param.10) | copy-start | bytes 3076
  7.4 4.4 %copy-start.7 = (f32[32]{0:T(128)S(1)}, f32[32]{0:T(128)}, u32[]{:S(2)}) copy-start(f32[32]{0:T(128)} %param.15) | copy-start | bytes 388
  7.4 4.4 %copy-start.2 = (bf16[256,32]{0,1:T(8,128)(2,1)S(1)}, bf16[256,32]{0,1:T(8,128)(2,1)}, u32[]{:S(2)}) copy-start(bf16[256,32]{0,1:T(8,128)(2,1)} %param.14) | copy-start | bytes 49156
  7.4 64.4 %all-gather.5.cloned.1.call-start = ((), (), s32[]{:S(2)}) async-start(), calls=%async_computation.2 | async-start | bytes 8912896 | tf_op jit(solution)/shard_map/all_gather | solution.py:46
  86.3 9.9 %copy-start.3 = (bf16[256,32]{0,1:T(8,128)(2,1)S(1)}, bf16[256,32]{0,1:T(8,128)(2,1)}, u32[]{:S(2)}) copy-start(bf16[256,32]{0,1:T(8,128)(2,1)} %param.12) | copy-start | bytes 49156
  86.3 65.8 %all-to-all-start = ((bf16[16,2,32768]{2,1,0:T(2,128)(2,1)}), bf16[16,2,32768]{2,1,0:T(2,128)(2,1)S(1)}, u32[]{:S(2)}, u32[]{:S(2)}) async-start(bf16[16,2,32768]{2,1,0:T(2,128)(2,1)} %reshape.40), calls=%async_computation | async-start | bytes 4194304 | tf_op jit(solution)/shard_map/all_to_all | solution.py:47
  96.0 99.7 %all-gather.3.cloned.1.call-start = ((), (), s32[]{:S(2)}) async-start(), calls=%async_computation.1 | async-start | bytes 2228224 | tf_op jit(solution)/shard_map/all_gather | solution.py:52
  204.1 24.4 %copy-start.4 = (f32[128]{0:T(128)S(1)}, f32[128]{0:T(128)}, u32[]{:S(2)}) copy-start(f32[128]{0:T(128)} %param.17) | copy-start | bytes 1540
Sparse Core Ops, SparseCore 0:
  14.3 57.5 all-gather.4
Sparse Core Ops, SparseCore 1:
  99.1 96.6 all-gather.2
where the time goes:
time: 249 us; the launch traced here: 247 us
  waiting for transfers between devices  128 us (51%)
  local copies, waits for them, and re-layouts  68.4 us (27%)
  matrix products  21.2 us (9%)
  between operations  15 us (6%)
  starting transfers between devices  9.96 us (4%)
  other arithmetic  4.27 us (2%)
    all_gather x1, waiting for transfers between devices, local(): right_all = lax.all_gather(second_major, 'res', axis=2, tiled=True)  57.7 us
    all_to_all x1, waiting for transfers between devices, local(): lax.all_to_all(right_all, 'seq', split_axis=2, concat_axis=0, tiled=True)  53.3 us
    reshape x1, local copies, waits for them, and re-layouts, local(): stacked = outer_mean.reshape(shard_positions, proj * proj, col_local)  24.4 us
    unnamed x18, local copies, waits for them, and re-layouts  23.4 us
    all_gather x1, waiting for transfers between devices, local(): left_all = lax.all_gather(first_factor, 'seq', axis=0, tiled=True)  17.4 us
    all_to_all x1, local copies, waits for them, and re-layouts, local(): lax.all_to_all(right_all, 'seq', split_axis=2, concat_axis=0, tiled=True)  11.5 us
    dot_general x1, matrix products, local(): lax.dot_general(stacked, final_map_matrix, (((1,), (0,)), ((), ())), pref...  11.3 us
    all_to_all x1, starting transfers between devices, local(): lax.all_to_all(right_all, 'seq', split_axis=2, concat_axis=0, tiled=True)  9.7 us
  transfers between devices with their start and end apart: 3, of which 3 were waited for; matrix products, arithmetic and copies ran while one was open for 12% of the time, Pallas kernels for 0%

commit v1 on v0

v1 whole, which is shorter than its diff:
```python
import jax
import jax.numpy as jnp
from jax import lax
from jax.experimental import pallas as pl
from jax.experimental.pallas import tpu as pltpu
from jax.sharding import PartitionSpec as P

MESH = pl.DeviceIdType.MESH
BF16, F32 = jnp.bfloat16, jnp.float32
SEQS, POS, CH, HID, CZ = 32, 64, 256, 32, 128
NQ = 16
PARTS = 4
PI = POS // PARTS
LANES = PI * HID
PIECES = 8
TOTAL = SEQS * NQ


def device(x, yl, c, h, z):
    return (x * 4 + yl * 2 + c, h * 8 + z)


def kernel(
    x_hbm, gain_hbm, shift_hbm, w1_hbm, b1_hbm, w2_hbm, b2_hbm, wf_hbm, bf_hbm, out_hbm,
    xv, gain, shift, w1, b1, w2, b2, wf, bf,
    normed0, normed1, tright, lrows, rown, rpart, lbuf, rbuf, lt, wfloat, wrows, wt, outer, obuf,
    in_sem, out_sem, lsend, lrecv, r0send, r0recv, r1send, r1recv, r2send, r2recv, r3send, r3recv,
):
    r, q = lax.axis_index("res"), lax.axis_index("seq")
    x, yl, c, h, z = r // 4, (r // 2) % 2, r % 2, q // 8, q % 8
    xp, xm, xo = (x + 1) % 4, (x + 3) % 4, (x + 2) % 4
    zp, zm = (z + 1) % 8, (z + 7) % 8
    half = (c + h + z + 1) % 2
    src_yl, src_c = (q // 2) % 2, q % 2
    piece = x * 2 + yl

    barrier = pltpu.get_barrier_semaphore()
    sources = [device(x, yl, c, h, zp), device(x, yl, c, h, zm), device(x, yl, c, 1 - h, z)]
    sources += [device(xp, yl, c, h, z), device(xm, yl, c, h, z), device(xo, yl, c, h, z)]
    sources += [device(x, 1 - yl, c, h, z), device(x, yl, 1 - c, h, z)]
    sources += [device(x, src_yl, src_c, half, k) for k in range(8)]
    for who in sources:
        pl.semaphore_signal(barrier, inc=1, device_id=who, device_id_type=MESH)

    loads = []
    for k, (src, dst) in enumerate([
        (x_hbm, xv), (gain_hbm, gain), (shift_hbm, shift), (w1_hbm, w1), (b1_hbm, b1),
        (w2_hbm, w2), (b2_hbm, b2), (wf_hbm, wf), (bf_hbm, bf),
    ]):
        loads.append(pltpu.make_async_copy(src, dst, in_sem.at[k]))
        loads[-1].start()
    for load in loads:
        load.wait()

    b2c = jnp.broadcast_to(b2[...].reshape(1, HID), (128, HID)).T
    b2c = jnp.concatenate([b2c] * 4, axis=1)
    g, o = gain[...].reshape(1, CH), shift[...].reshape(1, CH)

    def norm_step(b, _):
        v = xv[pl.ds(b * 8, 8)].reshape(8 * POS, CH).astype(F32)
        d = v - jnp.mean(v, axis=-1, keepdims=True)
        n = d * lax.rsqrt(jnp.mean(d * d, axis=-1, keepdims=True) + 1e-05) * g + o
        normed0[pl.ds(b * 512, 512), :] = n[:, :128]
        normed1[pl.ds(b * 512, 512), :] = n[:, 128:]
        t = lax.dot_general(w2[...], n.astype(BF16), (((1,), (1,)), ((), ())), preferred_element_type=F32) + b2c
        for u in range(4):
            tright[pl.ds((b * 4 + u) * HID, HID), :] = t[:, u * 128:(u + 1) * 128]
        return 0

    lax.fori_loop(0, SEQS // 8, norm_step, 0)
    low = lax.broadcasted_iota(jnp.int32, (16, 128), 1) < POS
    for t in range(HID // 2):
        a = tright[pl.ds(2 * t, 16, stride=HID), :]
        b = tright[pl.ds(2 * t + 1, 16, stride=HID), :]
        lane = (t % 2) * 128
        rown[t // 2, 0:16, lane:lane + 128] = jnp.where(low, a, pltpu.roll(b, POS, 1)).astype(BF16)
        rown[t // 2, 16:32, lane:lane + 128] = jnp.where(low, pltpu.roll(a, POS, 1), b).astype(BF16)

    pl.semaphore_wait(barrier, len(sources))

    pending = []

    def send(src, dst, ssem, rsem, who):
        copy = pltpu.make_async_remote_copy(
            src_ref=src, dst_ref=dst, send_sem=ssem, recv_sem=rsem, device_id=who, device_id_type=MESH
        )
        copy.start()
        pending.append(copy)

    def arrived(ref, sem):
        pltpu.make_async_remote_copy(
            src_ref=ref, dst_ref=ref, send_sem=sem, recv_sem=sem, device_id=device(x, yl, 1 - c, h, z),
            device_id_type=MESH,
        ).wait_recv()

    px, mx, ox = device(xp, yl, c, h, z), device(xm, yl, c, h, z), device(xo, yl, c, h, z)
    for n, (xx, who) in enumerate(((xp, px), (xm, mx), (xo, ox))):
        send(rown.at[pl.ds(2 * xx, 2)], rpart.at[x], r0send.at[n], r0recv.at[x], who)

    def scatter(n, xs, ref):
        hd = xs // 2
        for y2 in range(2):
            send(
                ref.at[y2], rbuf.at[2 * x + y2, q], r1send.at[2 * n + y2], r1recv.at[z],
                device(x, y2, (h + hd + c + 1) % 2, hd, (xs % 2) * 4 + yl * 2 + c),
            )

    scatter(0, x, rown.at[pl.ds(2 * x, 2)])

    lane4 = lax.broadcasted_iota(jnp.int32, (4 * CH, 128), 1) // HID
    row4 = lax.broadcasted_iota(jnp.int32, (4 * CH, 128), 0) // CH
    w1w = jnp.concatenate([w1[...].astype(F32).T] * 4, axis=1)
    w1w = jnp.where(lane4 == row4, jnp.concatenate([w1w] * 4, axis=0), 0.0).astype(BF16)
    b1w = jnp.concatenate([b1[...].reshape(1, HID)] * 4, axis=1)

    def chunk(side, d):
        hh = h if side == 0 else 1 - h
        return hh * 8 + (z + d + 8) % 8

    def lsend_to(p, k, idx, who):
        send(lbuf.at[p, idx], lbuf.at[p, idx], lsend.at[p, k], lrecv.at[p, idx], who)

    def lwait(p, side, d):
        idx = chunk(side, d)
        arrived(lbuf.at[p, idx], lrecv.at[p, idx])

    up, down, over = device(x, yl, c, h, zp), device(x, yl, c, h, zm), device(x, yl, c, 1 - h, z)

    for p in range(PARTS):
        for gl in range(PI // 4):
            for i4 in range(4):
                i = p * PI + gl * 4 + i4
                for lo in range(2):
                    for n, normed in enumerate((normed0, normed1)):
                        lane = i4 * CH + n * 128
                        lrows[gl * 32 + lo * 16:gl * 32 + lo * 16 + 16, lane:lane + 128] = normed[
                            pl.ds(lo * POS + i, 16, stride=2 * POS), :
                        ].astype(BF16)
        left = (jnp.dot(lrows[...], w1w, preferred_element_type=F32) + b1w).astype(BF16)
        for gl in range(PI // 4):
            lbuf[p, q, :, gl * 128:(gl + 1) * 128] = left[gl * 32:(gl + 1) * 32, :]
        lsend_to(p, 0, q, up)
        lsend_to(p, 4, q, down)
        lsend_to(p, 8, q, over)

    for n, xx in enumerate((xp, xm, xo)):
        arrived(rpart.at[xx], r0recv.at[xx])
        scatter(n + 1, xx, rpart.at[xx])

    for k in range(8):
        arrived(rbuf.at[piece, half * 8 + k], r1recv.at[k])

    def quarter(k, which):
        return rbuf.at[k, pl.ds(which * 8, 8)]

    def rsend(n, k, who):
        send(quarter(k, half), quarter(k, half), r2send.at[n], r2recv.at[k], who)

    def rsibling(n, k):
        send(quarter(k, half), quarter(k, half), r3send.at[n], r3recv.at[k], device(x, yl, 1 - c, h, z))

    def rwait(k):
        arrived(quarter(k, half), r2recv.at[k])

    rsend(0, piece, device(x, 1 - yl, c, h, z))
    rsend(1, piece, px)
    rsend(2, piece, mx)
    rsend(3, piece, ox)
    rsibling(0, piece)

    wfloat[...] = wf[...].astype(F32)
    for e in range(HID):
        wrows[(e // 2) * HID:(e // 2 + 1) * HID, (e % 2) * CZ:(e % 2 + 1) * CZ] = wfloat[pl.ds(e, HID, stride=HID), :]
    wt[...] = wrows[...].T.astype(BF16)
    bias = bf[...].reshape(1, CZ)

    def step1(p):
        lwait(p, 0, -1)
        lsend_to(p, 1, chunk(0, -1), up)
        lsend_to(p, 9, chunk(0, -1), over)
        lwait(p, 0, 1)
        lsend_to(p, 5, chunk(0, 1), down)
        lsend_to(p, 10, chunk(0, 1), over)

    def step2(p):
        lwait(p, 0, -2)
        lsend_to(p, 2, chunk(0, -2), up)
        lsend_to(p, 11, chunk(0, -2), over)
        lwait(p, 0, 2)
        lsend_to(p, 6, chunk(0, 2), down)
        lsend_to(p, 12, chunk(0, 2), over)

    def step3(p):
        lwait(p, 0, -3)
        lwait(p, 0, 3)
        if p % 2 == 0:
            lsend_to(p, 3, chunk(0, -3), up)
        else:
            lsend_to(p, 7, chunk(0, 3), down)
        lwait(p, 1, -2)
        lsend_to(p, 13, chunk(1, -2), up)
        lwait(p, 1, 2)
        lsend_to(p, 15, chunk(1, 2), down)

    def step4(p):
        lwait(p, 1, -3)
        lwait(p, 1, 3)
        if p % 2 == 1:
            lsend_to(p, 14, chunk(1, -3), up)
        else:
            lsend_to(p, 16, chunk(1, 3), down)

    def finish(p):
        for side, d in ((0, 4), (1, 0), (1, -1), (1, 1), (1, 4)):
            lwait(p, side, d)

    low2 = lax.broadcasted_iota(jnp.int32, (128, 128), 1) < POS

    def compute(p):
        for b in range(4):
            lt[:, b * 128:(b + 1) * 128] = lbuf[p, 4 * b:4 * b + 4].reshape(128, LANES).T

        def first(k, _):
            prod = jnp.dot(
                lt[...], rbuf[k].reshape(TOTAL, 256), preferred_element_type=F32
            ).astype(BF16)
            for i in range(PI):
                for t in range(2):
                    outer[i // 2, pl.ds((2 * k + t) * HID, HID), (i % 2) * 128:(i % 2 + 1) * 128] = prod[
                        i * HID:(i + 1) * HID, t * 128:(t + 1) * 128
                    ]
            return 0

        lax.fori_loop(0, PIECES, first, 0)

        def second(n, _):
            y = jnp.dot(wt[...], outer[n], preferred_element_type=F32)
            for i in range(2):
                both = jnp.where(low2, y[:CZ, i * 128:(i + 1) * 128], y[CZ:, i * 128:(i + 1) * 128]).T
                pair = (both[:POS] + both[POS:]) * (1.0 / TOTAL) + bias
                obuf[p * PI + 2 * n + i] = pair.astype(BF16)
            return 0

        lax.fori_loop(0, PI // 2, second, 0)
        copy = pltpu.make_async_copy(obuf.at[pl.ds(p * PI, PI)], out_hbm.at[pl.ds(p * PI, PI)], out_sem.at[p])
        copy.start()
        return copy

    for p in range(PARTS):
        step1(p)
    other = x * 2 + 1 - yl
    rwait(other)
    rsend(4, other, px)
    rsend(5, other, mx)
    rsend(6, other, ox)
    rsibling(1, other)
    for p in range(PARTS):
        step2(p)
    for n, xx in enumerate((xp, xm, xo)):
        rwait(xx * 2 + yl)
        rsibling(2 + n, xx * 2 + yl)
    for p in range(PARTS):
        step3(p)
    for n, xx in enumerate((xp, xm, xo)):
        rwait(xx * 2 + 1 - yl)
        rsibling(5 + n, xx * 2 + 1 - yl)
    for p in range(PARTS):
        step4(p)
    for k in range(PIECES):
        arrived(quarter(k, 1 - half), r3recv.at[k])
    stores = []
    for p in range(PARTS):
        finish(p)
        stores.append(compute(p))
    for copy in pending:
        copy.wait_send()
    for copy in stores:
        copy.wait()


def local(x, gain, shift, w1, b1, w2, b2, wf, bf):
    hbm = pl.BlockSpec(memory_space=pl.ANY)
    dma = pltpu.SemaphoreType.DMA
    return pl.pallas_call(
        kernel,
        out_shape=jax.ShapeDtypeStruct((POS, POS, CZ), BF16),
        in_specs=[hbm] * 9,
        out_specs=hbm,
        scratch_shapes=[
            pltpu.VMEM((SEQS, POS, CH), BF16), pltpu.VMEM((CH,), F32), pltpu.VMEM((CH,), F32),
            pltpu.VMEM((HID, CH), BF16), pltpu.VMEM((HID,), F32),
            pltpu.VMEM((HID, CH), BF16), pltpu.VMEM((HID,), F32),
            pltpu.VMEM((HID * HID, CZ), BF16), pltpu.VMEM((CZ,), F32),
            pltpu.VMEM((SEQS * POS, 128), F32), pltpu.VMEM((SEQS * POS, 128), F32),
            pltpu.VMEM((SEQS // 2 * HID, 128), F32),
            pltpu.VMEM((PI // 4 * SEQS, 4 * CH), BF16),
            pltpu.VMEM((PIECES, SEQS, 256), BF16),
            pltpu.VMEM((4, 2, SEQS, 256), BF16),
            pltpu.VMEM((PARTS, NQ, SEQS, LANES), BF16),
            pltpu.VMEM((PIECES, NQ, SEQS, 256), BF16),
            pltpu.VMEM((LANES, TOTAL), BF16),
            pltpu.VMEM((HID * HID, CZ), F32),
            pltpu.VMEM((HID * HID // 2, 2 * CZ), F32),
            pltpu.VMEM((2 * CZ, HID * HID // 2), BF16),
            pltpu.VMEM((PI // 2, HID * HID // 2, 256), BF16),
            pltpu.VMEM((POS, POS, CZ), BF16),
            dma((9,)), dma((PARTS,)), dma((PARTS, 17)), dma((PARTS, NQ)), dma((3,)), dma((4,)), dma((PIECES,)), dma((8,)),
            dma((7,)), dma((PIECES,)), dma((PIECES,)), dma((PIECES,)),
        ],
        compiler_params=pltpu.CompilerParams(
            collective_id=0, has_side_effects=True, vmem_limit_bytes=56 * 2**20
        ),
    )(x, gain, shift, w1.T, b1, w2.T, b2, wf, bf)


def solution(mesh):
    return jax.shard_map(
        local,
        mesh=mesh,
        in_specs=(P("seq", "res", None), P(), P(), P(), P(), P(), P(), P(), P()),
        out_specs=P("res", "seq", None),
        check_vma=False,
    )
```

time: 249 us -> 64.6 us (0.26)
  the two profiles are of different devices: /device:TPU:2 before, /device:TPU:39 now
where the time goes in v1:
time: 64.6 us; the launch traced here: 64.5 us
  Pallas kernels  62.2 us (96%)
  local copies, waits for them, and re-layouts  2.26 us (3%)
    pallas_call x1, Pallas kernels, local(): pl.pallas_call(kernel, out_shape=jax.ShapeDtypeStruct((POS, POS, CZ), BF1...  62.2 us
    unnamed x1, local copies, waits for them, and re-layouts  2.26 us

profile of v1, /device:TPU:39, one launch (start us, length us, event | category | flops | bytes accessed | tf_op | source)
XLA Modules:
  0.0 64.5 jit_solution(3929628212189681939)
XLA Ops:
  0.0 62.2 %shard_map.91 = bf16[64,64,128]{2,1,0:T(8,128)(2,1)} custom-call(bf16[32,64,256]{2,1,0:T(8,128)(2,1)} %x_hbm.1, f32[256]{0:T(256)} %gain_hbm.1, f32[256]{0:T(256)} %shift_hbm.1, bf16[32,256]{1,0:T(8,128)(2,1)} %bitcast.2, f32[32]{0:T(128)} %b1_hbm.1, bf16[32,256]{1,0:T(8,128)(2,1)} %bitcast.3, f32[32]{0:T(128)} %b2_hbm.1, bf16[1024,128]{1,0:T(8,128)(2,1)} %wf_hbm.1, ...), custom_call_target="tpu_custom_call" | custom-call | tf_op jit(solution)/shard_map/pallas_call | solution.py:284
  62.2 2.3 %copy.11 = bf16[64,64,128]{2,1,0:T(8,128)(2,1)} copy(bf16[64,64,128]{2,1,0:T(8,128)(2,1)} %shard_map.91) | data formatting | bytes 2097152

commit v2 on v1

--- a/solution.py
+++ b/solution.py
@@ -1,3 +1,5 @@
+import functools
+
 import jax
 import jax.numpy as jnp
 from jax import lax
@@ -9,6 +11,7 @@
 BF16, F32 = jnp.bfloat16, jnp.float32
 SEQS, POS, CH, HID, CZ = 32, 64, 256, 32, 128
 NQ = 16
+OWN, SKEW, LAST = 0.2, 0.65, 2.1
 PARTS = 4
 PI = POS // PARTS
 LANES = PI * HID
@@ -21,10 +24,10 @@
 
 
 def kernel(
-    x_hbm, gain_hbm, shift_hbm, w1_hbm, b1_hbm, w2_hbm, b2_hbm, wf_hbm, bf_hbm, out_hbm,
+    x_hbm, gain_hbm, shift_hbm, w1_hbm, b1_hbm, w2_hbm, b2_hbm, wf_hbm, bf_hbm, out,
     xv, gain, shift, w1, b1, w2, b2, wf, bf,
-    normed0, normed1, tright, lrows, rown, rpart, lbuf, rbuf, lt, wfloat, wrows, wt, outer, obuf,
-    in_sem, out_sem, lsend, lrecv, r0send, r0recv, r1send, r1recv, r2send, r2recv, r3send, r3recv,
+    normed0, normed1, tright, lrows, rown, rpart, lbuf, rbuf, lt, wfloat, wrows, wt, outer,
+    in_sem, lsend, lrecv, r0send, r0recv, r1send, r1recv, r2send, r2recv, r3send, r3recv,
 ):
     r, q = lax.axis_index("res"), lax.axis_index("seq")
     x, yl, c, h, z = r // 4, (r // 2) % 2, r % 2, q // 8, q % 8
@@ -126,7 +129,7 @@
 
     up, down, over = device(x, yl, c, h, zp), device(x, yl, c, h, zm), device(x, yl, c, 1 - h, z)
 
-    for p in range(PARTS):
+    def own(p):
         for gl in range(PI // 4):
             for i4 in range(4):
                 i = p * PI + gl * 4 + i4
@@ -143,30 +146,56 @@
         lsend_to(p, 4, q, down)
         lsend_to(p, 8, q, over)
 
-    for n, xx in enumerate((xp, xm, xo)):
-        arrived(rpart.at[xx], r0recv.at[xx])
-        scatter(n + 1, xx, rpart.at[xx])
-
-    for k in range(8):
-        arrived(rbuf.at[piece, half * 8 + k], r1recv.at[k])
-
-    def quarter(k, which):
+    other = x * 2 + 1 - yl
+    yld, sib = device(x, 1 - yl, c, h, z), device(x, yl, 1 - c, h, z)
+
+    def rows(k, zz):
+        return rbuf.at[k, half * 8 + zz]
+
+    def rsend(n, k, zz, who):
+        send(rows(k, zz), rows(k, zz), r2send.at[n, zz], r2recv.at[k, zz], who)
+
+    def rwait(k, zz):
+        arrived(rows(k, zz), r2recv.at[k, zz])
+
+    def eighth(k, which):
         return rbuf.at[k, pl.ds(which * 8, 8)]
 
-    def rsend(n, k, who):
-        send(quarter(k, half), quarter(k, half), r2send.at[n], r2recv.at[k], who)
-
     def rsibling(n, k):
-        send(quarter(k, half), quarter(k, half), r3send.at[n], r3recv.at[k], device(x, yl, 1 - c, h, z))
-
-    def rwait(k):
-        arrived(quarter(k, half), r2recv.at[k])
-
-    rsend(0, piece, device(x, 1 - yl, c, h, z))
-    rsend(1, piece, px)
-    rsend(2, piece, mx)
-    rsend(3, piece, ox)
-    rsibling(0, piece)
+        send(eighth(k, half), eighth(k, half), r3send.at[n], r3recv.at[k], sib)
+
+    def rgather(n, k):
+        for zz in range(8):
+            rwait(k, zz)
+        rsibling(n, k)
+
+    def r0():
+        for n, xx in enumerate((xp, xm, xo)):
+            arrived(rpart.at[xx], r0recv.at[xx])
+            scatter(n + 1, xx, rpart.at[xx])
+
+    def r1(d):
+        zz = (z + d + 8) % 8
+        arrived(rows(piece, zz), r1recv.at[zz])
+        rsend(0, piece, zz, yld)
+        rsend(1, piece, zz, px)
+        rsend(2, piece, zz, mx)
+        rsend(3, piece, zz, ox)
+
+    def ryl(d):
+        zz = (z + d + 8) % 8
+        rwait(other, zz)
+        rsend(4, other, zz, px)
+        rsend(5, other, zz, mx)
+
+    def rant(d):
+        zz = (z + d + 8) % 8
+        rwait(xo * 2 + yl, zz)
+        rsend(6, xo * 2 + yl, zz, yld)
+
+    def rsib():
+        for k in range(PIECES):
+            arrived(eighth(k, 1 - half), r3recv.at[k])
 
     wfloat[...] = wf[...].astype(F32)
     for e in range(HID):
@@ -174,7 +203,7 @@
     wt[...] = wrows[...].T.astype(BF16)
     bias = bf[...].reshape(1, CZ)
 
-    def step1(p):
+    def s1(p):
         lwait(p, 0, -1)
         lsend_to(p, 1, chunk(0, -1), up)
         lsend_to(p, 9, chunk(0, -1), over)
@@ -182,110 +211,122 @@
         lsend_to(p, 5, chunk(0, 1), down)
         lsend_to(p, 10, chunk(0, 1), over)
 
-    def step2(p):
+    def s2(p):
         lwait(p, 0, -2)
         lsend_to(p, 2, chunk(0, -2), up)
-        lsend_to(p, 11, chunk(0, -2), over)
+        if p % 2 == 0:
+            lsend_to(p, 11, chunk(0, -2), over)
         lwait(p, 0, 2)
         lsend_to(p, 6, chunk(0, 2), down)
-        lsend_to(p, 12, chunk(0, 2), over)
-
-    def step3(p):
+        if p % 2 == 1:
+            lsend_to(p, 11, chunk(0, 2), over)
+
+    def s3(p):
         lwait(p, 0, -3)
+        if p % 2 == 1:
+            lsend_to(p, 3, chunk(0, -3), up)
         lwait(p, 0, 3)
         if p % 2 == 0:
-            lsend_to(p, 3, chunk(0, -3), up)
+            lsend_to(p, 7, chunk(0, 3), down)
+
+    def c1(p):
+        if p % 2 == 1:
+            lwait(p, 1, -1)
+            lsend_to(p, 12, chunk(1, -1), up)
         else:
-            lsend_to(p, 7, chunk(0, 3), down)
+            lwait(p, 1, 1)
+            lsend_to(p, 12, chunk(1, 1), down)
+
+    def c2(p):
         lwait(p, 1, -2)
         lsend_to(p, 13, chunk(1, -2), up)
         lwait(p, 1, 2)
-        lsend_to(p, 15, chunk(1, 2), down)
-
-    def step4(p):
-        lwait(p, 1, -3)
-        lwait(p, 1, 3)
-        if p % 2 == 1:
-            lsend_to(p, 14, chunk(1, -3), up)
+        lsend_to(p, 14, chunk(1, 2), down)
+
+    def c3(p):
+        if p % 2 == 0:
+            lwait(p, 1, -3)
+            lsend_to(p, 15, chunk(1, -3), up)
         else:
-            lsend_to(p, 16, chunk(1, 3), down)
+            lwait(p, 1, 3)
+            lsend_to(p, 15, chunk(1, 3), down)
 
     def finish(p):
-        for side, d in ((0, 4), (1, 0), (1, -1), (1, 1), (1, 4)):
+        if p % 2 == 0:
+            last = (1, -1), (1, 3)
+        else:
+            last = (1, 1), (1, -3)
+        for side, d in ((0, 4), (1, 0), (1, 4)) + last:
             lwait(p, side, d)
 
     low2 = lax.broadcasted_iota(jnp.int32, (128, 128), 1) < POS
 
-    def compute(p):
-        for b in range(4):
-            lt[:, b * 128:(b + 1) * 128] = lbuf[p, 4 * b:4 * b + 4].reshape(128, LANES).T
-
-        def first(k, _):
-            prod = jnp.dot(
-                lt[...], rbuf[k].reshape(TOTAL, 256), preferred_element_type=F32
-            ).astype(BF16)
-            for i in range(PI):
-                for t in range(2):
-                    outer[i // 2, pl.ds((2 * k + t) * HID, HID), (i % 2) * 128:(i % 2 + 1) * 128] = prod[
-                        i * HID:(i + 1) * HID, t * 128:(t + 1) * 128
-                    ]
-            return 0
-
-        lax.fori_loop(0, PIECES, first, 0)
-
-        def second(n, _):
+    def compute(stage, p):
+        if stage == 0:
+            for b in range(4):
+                lt[:, b * 128:(b + 1) * 128] = lbuf[p, 4 * b:4 * b + 4].reshape(128, LANES).T
+        if stage < 2:
+            for k in range(stage * 4, stage * 4 + 4):
+                prod = jnp.dot(lt[...], rbuf[k].reshape(TOTAL, 256), preferred_element_type=F32).astype(BF16)
+                for i in range(PI):
+                    for t in range(2):
+                        outer[i // 2, (2 * k + t) * HID:(2 * k + t + 1) * HID, (i % 2) * 128:(i % 2 + 1) * 128] = prod[
+                            i * HID:(i + 1) * HID, t * 128:(t + 1) * 128
+                        ]
+            return
+        for n in range((stage - 2) * 4, (stage - 2) * 4 + 4):
             y = jnp.dot(wt[...], outer[n], preferred_element_type=F32)
             for i in range(2):
                 both = jnp.where(low2, y[:CZ, i * 128:(i + 1) * 128], y[CZ:, i * 128:(i + 1) * 128]).T
                 pair = (both[:POS] + both[POS:]) * (1.0 / TOTAL) + bias
-                obuf[p * PI + 2 * n + i] = pair.astype(BF16)
-            return 0
-
-        lax.fori_loop(0, PI // 2, second, 0)
-        copy = pltpu.make_async_copy(obuf.at[pl.ds(p * PI, PI)], out_hbm.at[pl.ds(p * PI, PI)], out_sem.at[p])
-        copy.start()
-        return copy
-
-    for p in range(PARTS):
-        step1(p)
-    other = x * 2 + 1 - yl
-    rwait(other)
-    rsend(4, other, px)
-    rsend(5, other, mx)
-    rsend(6, other, ox)
-    rsibling(1, other)
-    for p in range(PARTS):
-        step2(p)
-    for n, xx in enumerate((xp, xm, xo)):
-        rwait(xx * 2 + yl)
-        rsibling(2 + n, xx * 2 + yl)
-    for p in range(PARTS):
-        step3(p)
-    for n, xx in enumerate((xp, xm, xo)):
-        rwait(xx * 2 + 1 - yl)
-        rsibling(5 + n, xx * 2 + 1 - yl)
-    for p in range(PARTS):
-        step4(p)
-    for k in range(PIECES):
-        arrived(quarter(k, 1 - half), r3recv.at[k])
-    stores = []
-    for p in range(PARTS):
-        finish(p)
-        stores.append(compute(p))
+                out[p * PI + 2 * n + i] = pair.astype(BF16)
+
+    near = (0, 1, -1, 2, -2, 3, -3, 4)
+
+    def rsibling_own(_):
+        rsibling(0, piece)
+
+    steps = []
+
+    def plan(start, pitch, step, items):
+        for n, item in enumerate(items):
+            steps.append((start + pitch * n, functools.partial(step, item)))
+
+    steps.append((3.5, r0))
+    plan(6.5, 0.3, r1, near)
+    plan(9.0, 0, rsibling_own, [0])
+    plan(10.0, 0.4, ryl, near)
+    plan(13.1, 0, lambda _: rsibling(1, other), [0])
+    plan(11.0, 0.45, rant, near)
+    plan(14.5, 0, lambda _: rsibling(2, xo * 2 + yl), [0])
+    for n, (when, k) in enumerate(((14.6, xp * 2 + yl), (14.7, xm * 2 + yl), (17.0, xp * 2 + 1 - yl), (17.1, xm * 2 + 1 - yl), (17.6, xo * 2 + 1 - yl))):
+        steps.append((when, functools.partial(rgather, 3 + n, k)))
+    steps.append((18.4, rsib))
+    parts = range(PARTS)
+    plan(0.0, OWN, own, parts)
+    plan(3.9, SKEW, s1, parts)
+    plan(7.0, SKEW, s2, parts)
+    plan(8.1, SKEW, c1, parts)
+    plan(10.0, SKEW, s3, parts)
+    plan(12.6, SKEW, c2, parts)
+    plan(15.5, SKEW, c3, parts)
+    plan(18.5, LAST, finish, parts)
+    for n in range(4):
+        plan(18.5 + 0.01 + 0.5 * n, LAST, functools.partial(compute, n), parts)
+    for _, step in sorted(steps, key=lambda item: item[0]):
+        step()
     for copy in pending:
         copy.wait_send()
-    for copy in stores:
-        copy.wait()
 
 
 def local(x, gain, shift, w1, b1, w2, b2, wf, bf):
-    hbm = pl.BlockSpec(memory_space=pl.ANY)
+    args = [pltpu.with_memory_space_constraint(a, pltpu.HBM) for a in (x, gain, shift, w1.T, b1, w2.T, b2, wf, bf)]
     dma = pltpu.SemaphoreType.DMA
     return pl.pallas_call(
         kernel,
         out_shape=jax.ShapeDtypeStruct((POS, POS, CZ), BF16),
-        in_specs=[hbm] * 9,
-        out_specs=hbm,
+        in_specs=[pl.BlockSpec(memory_space=pltpu.HBM)] * 9,
+        out_specs=pl.BlockSpec(memory_space=pltpu.VMEM),
         scratch_shapes=[
             pltpu.VMEM((SEQS, POS, CH), BF16), pltpu.VMEM((CH,), F32), pltpu.VMEM((CH,), F32),
             pltpu.VMEM((HID, CH), BF16), pltpu.VMEM((HID,), F32),
@@ -303,14 +344,13 @@
             pltpu.VMEM((HID * HID // 2, 2 * CZ), F32),
             pltpu.VMEM((2 * CZ, HID * HID // 2), BF16),
             pltpu.VMEM((PI // 2, HID * HID // 2, 256), BF16),
-            pltpu.VMEM((POS, POS, CZ), BF16),
-            dma((9,)), dma((PARTS,)), dma((PARTS, 17)), dma((PARTS, NQ)), dma((3,)), dma((4,)), dma((PIECES,)), dma((8,)),
-            dma((7,)), dma((PIECES,)), dma((PIECES,)), dma((PIECES,)),
+            dma((9,)), dma((PARTS, 16)), dma((PARTS, NQ)), dma((3,)), dma((4,)), dma((PIECES,)), dma((8,)),
+            dma((7, 8)), dma((PIECES, 8)), dma((PIECES,)), dma((PIECES,)),
         ],
         compiler_params=pltpu.CompilerParams(
-            collective_id=0, has_side_effects=True, vmem_limit_bytes=56 * 2**20
+            collective_id=0, has_side_effects=True, vmem_limit_bytes=40 * 2**20
         ),
-    )(x, gain, shift, w1.T, b1, w2.T, b2, wf, bf)
+    )(*args)
 
 
 def solution(mesh):

time: 64.6 us -> 47.5 us (0.74)
  the two profiles are of different devices: /device:TPU:39 before, /device:TPU:9 now
where the time goes in v2:
time: 47.5 us; the launch traced here: 47.4 us
  Pallas kernels  46.4 us (98%)
  local copies, waits for them, and re-layouts  0.97 us (2%)
    pallas_call x1, Pallas kernels, local(): pl.pallas_call(kernel, out_shape=jax.ShapeDtypeStruct((POS, POS, CZ), BF1...  46.4 us
    unnamed x1, local copies, waits for them, and re-layouts  0.97 us

profile of v2, /device:TPU:9, one launch (start us, length us, event | category | flops | bytes accessed | tf_op | source)
XLA Modules:
  0.0 47.4 jit_solution(12327728940776382766)
XLA Ops:
  0.0 46.4 %shard_map.91 = bf16[64,64,128]{2,1,0:T(8,128)(2,1)S(1)} custom-call(bf16[32,64,256]{2,1,0:T(8,128)(2,1)} %x_hbm.1, f32[256]{0:T(256)} %gain_hbm.1, f32[256]{0:T(256)} %shift_hbm.1, bf16[32,256]{1,0:T(8,128)(2,1)} %bitcast.2, f32[32]{0:T(128)} %b1_hbm.1, bf16[32,256]{1,0:T(8,128)(2,1)} %bitcast.3, f32[32]{0:T(128)} %b2_hbm.1, bf16[1024,128]{1,0:T(8,128)(2,1)} %wf_hbm.1, ...), custom_call_target="tpu_custom_call" | custom-call | tf_op jit(solution)/shard_map/pallas_call | solution.py:325
  46.4 1.0 %copy.11 = bf16[64,64,128]{2,1,0:T(8,128)(2,1)} copy(bf16[64,64,128]{2,1,0:T(8,128)(2,1)S(1)} %shard_map.91) | data formatting | bytes 2097152

commit v3 on v2

--- a/solution.py
+++ b/solution.py
@@ -11,10 +11,13 @@
 BF16, F32 = jnp.bfloat16, jnp.float32
 SEQS, POS, CH, HID, CZ = 32, 64, 256, 32, 128
 NQ = 16
-OWN, SKEW, LAST = 0.2, 0.65, 2.1
+CROSS = (0, 0, 0, 0)
+RG = 2
 PARTS = 4
 PI = POS // PARTS
 LANES = PI * HID
+GROUPS = 1
+GI = POS // GROUPS
 PIECES = 8
 TOTAL = SEQS * NQ
 
@@ -26,8 +29,8 @@
 def kernel(
     x_hbm, gain_hbm, shift_hbm, w1_hbm, b1_hbm, w2_hbm, b2_hbm, wf_hbm, bf_hbm, out,
     xv, gain, shift, w1, b1, w2, b2, wf, bf,
-    normed0, normed1, tright, lrows, rown, rpart, lbuf, rbuf, lt, wfloat, wrows, wt, outer,
-    in_sem, lsend, lrecv, r0send, r0recv, r1send, r1recv, r2send, r2recv, r3send, r3recv,
+    normed0, normed1, tright, lrows, rown, rpart, lbuf, rbuf, lt, wfloat, wrows, wt, outer, obuf,
+    in_sem, out_sem, lsend, lrecv, r0send, r0recv, r1send, r1recv, r2send, r2recv, r3send, r3recv,
 ):
     r, q = lax.axis_index("res"), lax.axis_index("seq")
     x, yl, c, h, z = r // 4, (r // 2) % 2, r % 2, q // 8, q % 8
@@ -50,17 +53,22 @@
         (x_hbm, xv), (gain_hbm, gain), (shift_hbm, shift), (w1_hbm, w1), (b1_hbm, b1),
         (w2_hbm, w2), (b2_hbm, b2), (wf_hbm, wf), (bf_hbm, bf),
     ]):
-        loads.append(pltpu.make_async_copy(src, dst, in_sem.at[k]))
-        loads[-1].start()
-    for load in loads:
+        for n in range(4 if k == 0 else 1):
+            if k == 0:
+                src, dst = x_hbm.at[pl.ds(n * 8, 8)], xv.at[pl.ds(n * 8, 8)]
+            loads.append(pltpu.make_async_copy(src, dst, in_sem.at[len(loads)]))
+            loads[-1].start()
+    xloads, loads = loads[:4], loads[3:]
+    for load in loads[1:7]:
         load.wait()
 
     b2c = jnp.broadcast_to(b2[...].reshape(1, HID), (128, HID)).T
     b2c = jnp.concatenate([b2c] * 4, axis=1)
     g, o = gain[...].reshape(1, CH), shift[...].reshape(1, CH)
 
-    def norm_step(b, _):
-        v = xv[pl.ds(b * 8, 8)].reshape(8 * POS, CH).astype(F32)
+    def norm_step(b):
+        xloads[b].wait()
+        v = xv[b * 8:b * 8 + 8].reshape(8 * POS, CH).astype(F32)
         d = v - jnp.mean(v, axis=-1, keepdims=True)
         n = d * lax.rsqrt(jnp.mean(d * d, axis=-1, keepdims=True) + 1e-05) * g + o
         normed0[pl.ds(b * 512, 512), :] = n[:, :128]
@@ -68,9 +76,9 @@
         t = lax.dot_general(w2[...], n.astype(BF16), (((1,), (1,)), ((), ())), preferred_element_type=F32) + b2c
         for u in range(4):
             tright[pl.ds((b * 4 + u) * HID, HID), :] = t[:, u * 128:(u + 1) * 128]
-        return 0
-
-    lax.fori_loop(0, SEQS // 8, norm_step, 0)
+
+    for b in range(SEQS // 8):
+        norm_step(b)
     low = lax.broadcasted_iota(jnp.int32, (16, 128), 1) < POS
     for t in range(HID // 2):
         a = tright[pl.ds(2 * t, 16, stride=HID), :]
@@ -79,6 +87,12 @@
         rown[t // 2, 0:16, lane:lane + 128] = jnp.where(low, a, pltpu.roll(b, POS, 1)).astype(BF16)
         rown[t // 2, 16:32, lane:lane + 128] = jnp.where(low, pltpu.roll(a, POS, 1), b).astype(BF16)
 
+    lane4 = lax.broadcasted_iota(jnp.int32, (4 * CH, 128), 1) // HID
+    row4 = lax.broadcasted_iota(jnp.int32, (4 * CH, 128), 0) // CH
+    w1w = jnp.concatenate([w1[...].astype(F32).T] * 4, axis=1)
+    w1w = jnp.where(lane4 == row4, jnp.concatenate([w1w] * 4, axis=0), 0.0).astype(BF16)
+    b1w = jnp.concatenate([b1[...].reshape(1, HID)] * 4, axis=1)
+
     pl.semaphore_wait(barrier, len(sources))
 
     pending = []
@@ -109,12 +123,6 @@
             )
 
     scatter(0, x, rown.at[pl.ds(2 * x, 2)])
-
-    lane4 = lax.broadcasted_iota(jnp.int32, (4 * CH, 128), 1) // HID
-    row4 = lax.broadcasted_iota(jnp.int32, (4 * CH, 128), 0) // CH
-    w1w = jnp.concatenate([w1[...].astype(F32).T] * 4, axis=1)
-    w1w = jnp.where(lane4 == row4, jnp.concatenate([w1w] * 4, axis=0), 0.0).astype(BF16)
-    b1w = jnp.concatenate([b1[...].reshape(1, HID)] * 4, axis=1)
 
     def chunk(side, d):
         hh = h if side == 0 else 1 - h
@@ -149,8 +157,8 @@
     other = x * 2 + 1 - yl
     yld, sib = device(x, 1 - yl, c, h, z), device(x, yl, 1 - c, h, z)
 
-    def rows(k, zz):
-        return rbuf.at[k, half * 8 + zz]
+    def rows(k, m):
+        return rbuf.at[k, pl.ds(half * 8 + m * RG, RG)]
 
     def rsend(n, k, zz, who):
         send(rows(k, zz), rows(k, zz), r2send.at[n, zz], r2recv.at[k, zz], who)
@@ -165,9 +173,11 @@
         send(eighth(k, half), eighth(k, half), r3send.at[n], r3recv.at[k], sib)
 
     def rgather(n, k):
-        for zz in range(8):
-            rwait(k, zz)
+        for m in range(8 // RG):
+            rwait(k, m)
         rsibling(n, k)
+
+    near = {1: (0, 1, -1, 2, -2, 3, -3, 4), 2: (0, 1, -1, 2), 4: (0, 1), 8: (0,)}[RG]
 
     def r0():
         for n, xx in enumerate((xp, xm, xo)):
@@ -175,33 +185,43 @@
             scatter(n + 1, xx, rpart.at[xx])
 
     def r1(d):
-        zz = (z + d + 8) % 8
-        arrived(rows(piece, zz), r1recv.at[zz])
+        zz = (z // RG + d + 8) % (8 // RG)
+        for n in range(RG):
+            arrived(rbuf.at[piece, half * 8 + zz * RG + n], r1recv.at[zz * RG + n])
         rsend(0, piece, zz, yld)
         rsend(1, piece, zz, px)
         rsend(2, piece, zz, mx)
         rsend(3, piece, zz, ox)
+        if d == near[-1]:
+            rsibling(0, piece)
 
     def ryl(d):
-        zz = (z + d + 8) % 8
+        zz = (z // RG + d + 8) % (8 // RG)
         rwait(other, zz)
         rsend(4, other, zz, px)
         rsend(5, other, zz, mx)
+        if d == near[-1]:
+            rsibling(1, other)
 
     def rant(d):
-        zz = (z + d + 8) % 8
+        zz = (z // RG + d + 8) % (8 // RG)
         rwait(xo * 2 + yl, zz)
         rsend(6, xo * 2 + yl, zz, yld)
+        if d == near[-1]:
+            rsibling(2, xo * 2 + yl)
 
     def rsib():
         for k in range(PIECES):
             arrived(eighth(k, 1 - half), r3recv.at[k])
 
-    wfloat[...] = wf[...].astype(F32)
-    for e in range(HID):
-        wrows[(e // 2) * HID:(e // 2 + 1) * HID, (e % 2) * CZ:(e % 2 + 1) * CZ] = wfloat[pl.ds(e, HID, stride=HID), :]
-    wt[...] = wrows[...].T.astype(BF16)
-    bias = bf[...].reshape(1, CZ)
+    def weights():
+        loads[7].wait()
+        loads[8].wait()
+        wfloat[...] = wf[...].astype(F32)
+        for e in range(HID):
+            wrows[(e // 2) * HID:(e // 2 + 1) * HID, (e % 2) * CZ:(e % 2 + 1) * CZ] = wfloat[pl.ds(e, HID, stride=HID), :]
+        wt[...] = wrows[...].T.astype(BF16)
+
 
     def s1(p):
         lwait(p, 0, -1)
@@ -211,15 +231,18 @@
         lsend_to(p, 5, chunk(0, 1), down)
         lsend_to(p, 10, chunk(0, 1), over)
 
+    def crosses(p, d):
+        return CROSS[p] == 2 or CROSS[p] == 1 and (d < 0) == (p % 2 == 0)
+
     def s2(p):
         lwait(p, 0, -2)
         lsend_to(p, 2, chunk(0, -2), up)
-        if p % 2 == 0:
+        if crosses(p, -2):
             lsend_to(p, 11, chunk(0, -2), over)
         lwait(p, 0, 2)
         lsend_to(p, 6, chunk(0, 2), down)
-        if p % 2 == 1:
-            lsend_to(p, 11, chunk(0, 2), over)
+        if crosses(p, 2):
+            lsend_to(p, 16, chunk(0, 2), over)
 
     def s3(p):
         lwait(p, 0, -3)
@@ -230,12 +253,12 @@
             lsend_to(p, 7, chunk(0, 3), down)
 
     def c1(p):
-        if p % 2 == 1:
+        if not crosses(p, -2):
             lwait(p, 1, -1)
             lsend_to(p, 12, chunk(1, -1), up)
-        else:
+        if not crosses(p, 2):
             lwait(p, 1, 1)
-            lsend_to(p, 12, chunk(1, 1), down)
+            lsend_to(p, 17, chunk(1, 1), down)
 
     def c2(p):
         lwait(p, 1, -2)
@@ -252,39 +275,43 @@
             lsend_to(p, 15, chunk(1, 3), down)
 
     def finish(p):
-        if p % 2 == 0:
-            last = (1, -1), (1, 3)
-        else:
-            last = (1, 1), (1, -3)
-        for side, d in ((0, 4), (1, 0), (1, 4)) + last:
+        for side, d in ((0, 4), (1, 0), (1, 4), (1, 3 if p % 2 == 0 else -3)):
             lwait(p, side, d)
+        for d in (-1, 1):
+            if crosses(p, 2 * d):
+                lwait(p, 1, d)
 
     low2 = lax.broadcasted_iota(jnp.int32, (128, 128), 1) < POS
 
-    def compute(stage, p):
-        if stage == 0:
-            for b in range(4):
-                lt[:, b * 128:(b + 1) * 128] = lbuf[p, 4 * b:4 * b + 4].reshape(128, LANES).T
-        if stage < 2:
-            for k in range(stage * 4, stage * 4 + 4):
-                prod = jnp.dot(lt[...], rbuf[k].reshape(TOTAL, 256), preferred_element_type=F32).astype(BF16)
-                for i in range(PI):
-                    for t in range(2):
-                        outer[i // 2, (2 * k + t) * HID:(2 * k + t + 1) * HID, (i % 2) * 128:(i % 2 + 1) * 128] = prod[
-                            i * HID:(i + 1) * HID, t * 128:(t + 1) * 128
-                        ]
-            return
-        for n in range((stage - 2) * 4, (stage - 2) * 4 + 4):
-            y = jnp.dot(wt[...], outer[n], preferred_element_type=F32)
-            for i in range(2):
-                both = jnp.where(low2, y[:CZ, i * 128:(i + 1) * 128], y[CZ:, i * 128:(i + 1) * 128]).T
-                pair = (both[:POS] + both[POS:]) * (1.0 / TOTAL) + bias
-                out[p * PI + 2 * n + i] = pair.astype(BF16)
-
-    near = (0, 1, -1, 2, -2, 3, -3, 4)
-
-    def rsibling_own(_):
-        rsibling(0, piece)
+    def turn(p):
+        for b in range(4):
+            for n in range(0, GI * HID, min(GI * HID, LANES)):
+                part, lane = divmod(p * GI * HID + n, LANES)
+                width = min(GI * HID, LANES)
+                lt[p % 2, n:n + width, b * 128:(b + 1) * 128] = (
+                    lbuf[part, 4 * b:4 * b + 4, :, lane:lane + width].reshape(128, width).T
+                )
+
+    def multiply(p, k):
+        prod = jnp.dot(lt[p % 2], rbuf[k].reshape(TOTAL, 256), preferred_element_type=F32).astype(BF16)
+        for i in range(GI):
+            for t in range(2):
+                outer[p % 2, i // 2, (2 * k + t) * HID:(2 * k + t + 1) * HID, (i % 2) * 128:(i % 2 + 1) * 128] = prod[
+                    i * HID:(i + 1) * HID, t * 128:(t + 1) * 128
+                ]
+
+    def project(p, n):
+        y = jnp.dot(wt[...], outer[p % 2, n], preferred_element_type=F32)
+        for i in range(2):
+            both = jnp.where(low2, y[:CZ, i * 128:(i + 1) * 128], y[CZ:, i * 128:(i + 1) * 128]).T
+            pair = (both[:POS] + both[POS:]) * (1.0 / TOTAL) + bf[...].reshape(1, CZ)
+            obuf[p * GI + 2 * n + i] = pair.astype(BF16)
+
+    def store(p):
+        copy = pltpu.make_async_copy(obuf.at[pl.ds(p * GI, GI)], out.at[pl.ds(p * GI, GI)], out_sem.at[p])
+        copy.start()
+        return copy
+
 
     steps = []
 
@@ -293,28 +320,43 @@
             steps.append((start + pitch * n, functools.partial(step, item)))
 
     steps.append((3.5, r0))
-    plan(6.5, 0.3, r1, near)
-    plan(9.0, 0, rsibling_own, [0])
-    plan(10.0, 0.4, ryl, near)
-    plan(13.1, 0, lambda _: rsibling(1, other), [0])
-    plan(11.0, 0.45, rant, near)
-    plan(14.5, 0, lambda _: rsibling(2, xo * 2 + yl), [0])
+    plan(8.0 + 0.15 * (RG - 1), 0.3 * RG, r1, near)
+    plan(12.0, 0.4 * RG, ryl, near)
+    plan(14.0, 0.45 * RG, rant, near)
     for n, (when, k) in enumerate(((14.6, xp * 2 + yl), (14.7, xm * 2 + yl), (17.0, xp * 2 + 1 - yl), (17.1, xm * 2 + 1 - yl), (17.6, xo * 2 + 1 - yl))):
         steps.append((when, functools.partial(rgather, 3 + n, k)))
     steps.append((18.4, rsib))
     parts = range(PARTS)
-    plan(0.0, OWN, own, parts)
-    plan(3.9, SKEW, s1, parts)
-    plan(7.0, SKEW, s2, parts)
-    plan(8.1, SKEW, c1, parts)
-    plan(10.0, SKEW, s3, parts)
-    plan(12.6, SKEW, c2, parts)
-    plan(15.5, SKEW, c3, parts)
-    plan(18.5, LAST, finish, parts)
-    for n in range(4):
-        plan(18.5 + 0.01 + 0.5 * n, LAST, functools.partial(compute, n), parts)
+    plan(0.0, 0.8 / PARTS, own, parts)
+    steps.append((1.0, weights))
+    pitch = 2.6 / PARTS
+    plan(3.9, pitch, s1, parts)
+    plan(7.0, pitch, s2, parts)
+    plan(8.1, pitch, c1, parts)
+    plan(10.0, pitch, s3, parts)
+    plan(12.6, pitch, c2, parts)
+    plan(15.5, pitch, c3, parts)
     for _, step in sorted(steps, key=lambda item: item[0]):
         step()
+    stores = []
+    each = GI // 2 // PIECES
+    for p in range(GROUPS):
+        for n in range(PARTS):
+            if n * GROUPS // PARTS == p:
+                finish(n)
+        turn(p)
+        for n in range(PIECES):
+            multiply(p, n)
+            if p > 0:
+                for m in range(each):
+                    project(p - 1, n * each + m)
+        if p > 0:
+            stores.append(store(p - 1))
+    for n in range(GI // 2):
+        project(GROUPS - 1, n)
+    stores.append(store(GROUPS - 1))
+    for copy in stores:
+        copy.wait()
     for copy in pending:
         copy.wait_send()
 
@@ -326,7 +368,7 @@
         kernel,
         out_shape=jax.ShapeDtypeStruct((POS, POS, CZ), BF16),
         in_specs=[pl.BlockSpec(memory_space=pltpu.HBM)] * 9,
-        out_specs=pl.BlockSpec(memory_space=pltpu.VMEM),
+        out_specs=pl.BlockSpec(memory_space=pl.ANY),
         scratch_shapes=[
             pltpu.VMEM((SEQS, POS, CH), BF16), pltpu.VMEM((CH,), F32), pltpu.VMEM((CH,), F32),
             pltpu.VMEM((HID, CH), BF16), pltpu.VMEM((HID,), F32),
@@ -339,12 +381,13 @@
             pltpu.VMEM((4, 2, SEQS, 256), BF16),
             pltpu.VMEM((PARTS, NQ, SEQS, LANES), BF16),
             pltpu.VMEM((PIECES, NQ, SEQS, 256), BF16),
-            pltpu.VMEM((LANES, TOTAL), BF16),
+            pltpu.VMEM((2, GI * HID, TOTAL), BF16),
             pltpu.VMEM((HID * HID, CZ), F32),
             pltpu.VMEM((HID * HID // 2, 2 * CZ), F32),
             pltpu.VMEM((2 * CZ, HID * HID // 2), BF16),
-            pltpu.VMEM((PI // 2, HID * HID // 2, 256), BF16),
-            dma((9,)), dma((PARTS, 16)), dma((PARTS, NQ)), dma((3,)), dma((4,)), dma((PIECES,)), dma((8,)),
+            pltpu.VMEM((2, GI // 2, HID * HID // 2, 256), BF16),
+            pltpu.VMEM((POS, POS, CZ), BF16),
+            dma((12,)), dma((GROUPS,)), dma((PARTS, 18)), dma((PARTS, NQ)), dma((3,)), dma((4,)), dma((PIECES,)), dma((8,)),
             dma((7, 8)), dma((PIECES, 8)), dma((PIECES,)), dma((PIECES,)),
         ],
         compiler_params=pltpu.CompilerParams(

time: 47.5 us -> 46.1 us (0.971)
  the two profiles are of different devices: /device:TPU:9 before, /device:TPU:2 now
where the time goes in v3:
time: 46.1 us; the launch traced here: 45.6 us
  Pallas kernels  44.6 us (97%)
  local copies, waits for them, and re-layouts  0.97 us (2%)
    pallas_call x1, Pallas kernels, local(): pl.pallas_call(kernel, out_shape=jax.ShapeDtypeStruct((POS, POS, CZ), BF1...  44.6 us
    unnamed x1, local copies, waits for them, and re-layouts  0.97 us

profile of v3, /device:TPU:2, one launch (start us, length us, event | category | flops | bytes accessed | tf_op | source)
XLA Modules:
  0.0 45.6 jit_solution(15219680272128806279)
XLA Ops:
  0.0 44.6 %shard_map.91 = bf16[64,64,128]{2,1,0:T(8,128)(2,1)S(1)} custom-call(bf16[32,64,256]{2,1,0:T(8,128)(2,1)} %x_hbm.1, f32[256]{0:T(256)} %gain_hbm.1, f32[256]{0:T(256)} %shift_hbm.1, bf16[32,256]{1,0:T(8,128)(2,1)} %bitcast.2, f32[32]{0:T(128)} %b1_hbm.1, bf16[32,256]{1,0:T(8,128)(2,1)} %bitcast.3, f32[32]{0:T(128)} %b2_hbm.1, bf16[1024,128]{1,0:T(8,128)(2,1)} %wf_hbm.1, ...), custom_call_target="tpu_custom_call" | custom-call | tf_op jit(solution)/shard_map/pallas_call | solution.py:367
  44.6 1.0 %copy.11 = bf16[64,64,128]{2,1,0:T(8,128)(2,1)} copy(bf16[64,64,128]{2,1,0:T(8,128)(2,1)S(1)} %shard_map.91) | data formatting | bytes 2097152

commit v4 on v3

--- a/solution.py
+++ b/solution.py
@@ -29,8 +29,8 @@
 def kernel(
     x_hbm, gain_hbm, shift_hbm, w1_hbm, b1_hbm, w2_hbm, b2_hbm, wf_hbm, bf_hbm, out,
     xv, gain, shift, w1, b1, w2, b2, wf, bf,
-    normed0, normed1, tright, lrows, rown, rpart, lbuf, rbuf, lt, wfloat, wrows, wt, outer, obuf,
-    in_sem, out_sem, lsend, lrecv, r0send, r0recv, r1send, r1recv, r2send, r2recv, r3send, r3recv,
+    normed0, normed1, tright, lrows, rown, rpart, lbuf, rbuf, lt, wfloat, wrows, wt, outer,
+    in_sem, lsend, lrecv, r0send, r0recv, r1send, r1recv, r2send, r2recv, r3send, r3recv,
 ):
     r, q = lax.axis_index("res"), lax.axis_index("seq")
     x, yl, c, h, z = r // 4, (r // 2) % 2, r % 2, q // 8, q % 8
@@ -305,12 +305,7 @@
         for i in range(2):
             both = jnp.where(low2, y[:CZ, i * 128:(i + 1) * 128], y[CZ:, i * 128:(i + 1) * 128]).T
             pair = (both[:POS] + both[POS:]) * (1.0 / TOTAL) + bf[...].reshape(1, CZ)
-            obuf[p * GI + 2 * n + i] = pair.astype(BF16)
-
-    def store(p):
-        copy = pltpu.make_async_copy(obuf.at[pl.ds(p * GI, GI)], out.at[pl.ds(p * GI, GI)], out_sem.at[p])
-        copy.start()
-        return copy
+            out[p * GI + 2 * n + i] = pair.astype(BF16)
 
 
     steps = []
@@ -338,7 +333,6 @@
     plan(15.5, pitch, c3, parts)
     for _, step in sorted(steps, key=lambda item: item[0]):
         step()
-    stores = []
     each = GI // 2 // PIECES
     for p in range(GROUPS):
         for n in range(PARTS):
@@ -350,13 +344,8 @@
             if p > 0:
                 for m in range(each):
                     project(p - 1, n * each + m)
-        if p > 0:
-            stores.append(store(p - 1))
     for n in range(GI // 2):
         project(GROUPS - 1, n)
-    stores.append(store(GROUPS - 1))
-    for copy in stores:
-        copy.wait()
     for copy in pending:
         copy.wait_send()
 
@@ -368,7 +357,7 @@
         kernel,
         out_shape=jax.ShapeDtypeStruct((POS, POS, CZ), BF16),
         in_specs=[pl.BlockSpec(memory_space=pltpu.HBM)] * 9,
-        out_specs=pl.BlockSpec(memory_space=pl.ANY),
+        out_specs=pl.BlockSpec(memory_space=pltpu.VMEM),
         scratch_shapes=[
             pltpu.VMEM((SEQS, POS, CH), BF16), pltpu.VMEM((CH,), F32), pltpu.VMEM((CH,), F32),
             pltpu.VMEM((HID, CH), BF16), pltpu.VMEM((HID,), F32),
@@ -386,8 +375,7 @@
             pltpu.VMEM((HID * HID // 2, 2 * CZ), F32),
             pltpu.VMEM((2 * CZ, HID * HID // 2), BF16),
             pltpu.VMEM((2, GI // 2, HID * HID // 2, 256), BF16),
-            pltpu.VMEM((POS, POS, CZ), BF16),
-            dma((12,)), dma((GROUPS,)), dma((PARTS, 18)), dma((PARTS, NQ)), dma((3,)), dma((4,)), dma((PIECES,)), dma((8,)),
+            dma((12,)), dma((PARTS, 18)), dma((PARTS, NQ)), dma((3,)), dma((4,)), dma((PIECES,)), dma((8,)),
             dma((7, 8)), dma((PIECES, 8)), dma((PIECES,)), dma((PIECES,)),
         ],
         compiler_params=pltpu.CompilerParams(

time: 46.1 us -> 46 us (level)
  no operation moved by 1% of the time
where the time goes in v4:
time: 46 us; the launch traced here: 45.5 us
  Pallas kernels  44.5 us (97%)
  local copies, waits for them, and re-layouts  0.97 us (2%)
    pallas_call x1, Pallas kernels, local(): pl.pallas_call(kernel, out_shape=jax.ShapeDtypeStruct((POS, POS, CZ), BF1...  44.5 us
    unnamed x1, local copies, waits for them, and re-layouts  0.97 us

profile of v4, /device:TPU:2, one launch (start us, length us, event | category | flops | bytes accessed | tf_op | source)
XLA Modules:
  0.0 45.5 jit_solution(2843586480352818574)
XLA Ops:
  0.0 44.5 %shard_map.91 = bf16[64,64,128]{2,1,0:T(8,128)(2,1)S(1)} custom-call(bf16[32,64,256]{2,1,0:T(8,128)(2,1)} %x_hbm.1, f32[256]{0:T(256)} %gain_hbm.1, f32[256]{0:T(256)} %shift_hbm.1, bf16[32,256]{1,0:T(8,128)(2,1)} %bitcast.2, f32[32]{0:T(128)} %b1_hbm.1, bf16[32,256]{1,0:T(8,128)(2,1)} %bitcast.3, f32[32]{0:T(128)} %b2_hbm.1, bf16[1024,128]{1,0:T(8,128)(2,1)} %wf_hbm.1, ...), custom_call_target="tpu_custom_call" | custom-call | tf_op jit(solution)/shard_map/pallas_call | solution.py:356
  44.5 1.0 %copy.11 = bf16[64,64,128]{2,1,0:T(8,128)(2,1)} copy(bf16[64,64,128]{2,1,0:T(8,128)(2,1)S(1)} %shard_map.91) | data formatting | bytes 2097152
